TPU v7x, 512 devices: a whole 4x8x8 slice. The times are simulated.
512 devices in a mesh: lat: 8 (over z_lo, core), lon: 64 (over z_hi, x, y).
Axes of the slice: x: 4, y: 8, z: 8 (z_hi: 2, z_lo: 4; z = z_hi * 4 + z_lo), core: 2. Of those that a mesh axis runs over, the one named last changes fastest.
Arguments:
- background_state: bfloat16 [18, 5760, 1024], P(None, 'lon', 'lat'), may hold values from -6 to 6
- perturbation: bfloat16 [18, 5760, 1024], P(None, 'lon', 'lat'), may hold values from -16 to 16
- surface_pattern_index: int32 [5760, 1024], P('lon', 'lat'), may hold values from 0 to 15
- surface_amplitude_table: float32 [16], replicated, may hold values from -4 to 4
- cutoff: int32 [1024], P('lat'), may hold values from 4 to 64, as said below
- zonal_row_weight: float32 [1024], P('lat'), may hold values from 0.5 to 2
- diffusivity: float32 [18], replicated, may hold values from 0.04 to 0.25
- input_weight: bfloat16 [48, 18], replicated, may hold values from -1.5 to 1.5
- bias: float32 [48], replicated, may hold values from -4 to 4
- output_weight: float32 [18, 48], replicated, may hold values from -0.875 to 0.875
Outputs:
- tangent: bfloat16 [18, 5760, 1024], P(None, 'lon', 'lat')
- gradient: bfloat16 [18, 5760, 1024], P(None, 'lon', 'lat')
Inputs may be any that keep to these rules, and one draw needn't show every extreme that they name: Rows 64 or more rows away from both ends of the grid have cutoff 64; the first and last rows have cutoff 4; a row d < 64 rows from the nearer end has cutoff at least 4 + (d * 60) // 64.
All inputs are finite; a program needn't handle non-finite values.
Results may differ from a plain program's by a relative error of at most 0.001.
Values sent between devices are 32-bit elements; how exact they have to be, the bound alone decides.
A program may use at most 64 MiB of HBM per device.

v0:
```python
import math
import jax
import jax.numpy as jnp
from jax import lax
from jax.sharding import PartitionSpec as P

LONGITUDE_COUNT = 5760
KW = 64
POLAR = 64
TOP_PRECISION = lax.Precision.HIGHEST


def padded(x, sides, width, wrap):
    for axis, dim in sides:
        count, length = (lax.axis_size(axis), x.shape[dim])
        up = [(i, (i + 1) % count) for i in range(count if wrap else count - 1)]
        down = [(j, i) for i, j in up]
        last = lax.slice_in_dim(x, length - width, length, axis=dim)
        leading = lax.slice_in_dim(x, 0, width, axis=dim)
        before = lax.ppermute(last, axis, up)
        after = lax.ppermute(leading, axis, down)
        x = jnp.concatenate([before, x, after], axis=dim)
    return x


def spectral_table(longitudes):
    wave_numbers = jnp.arange(1, KW + 1, dtype=jnp.int32)
    phase_index = longitudes[:, None] * wave_numbers[None, :] % LONGITUDE_COUNT
    angles = phase_index.astype(jnp.float32) * (2.0 * math.pi / LONGITUDE_COUNT)
    return jnp.concatenate([jnp.cos(angles), jnp.sin(angles)], axis=1)


def removal_weights(cutoff):
    wave_numbers = jnp.arange(1, KW + 1, dtype=jnp.float32)[:, None]
    cut_limit = cutoff.astype(jnp.float32)[None, :]
    cut_ratio = cut_limit / wave_numbers
    damping = jnp.where(wave_numbers > cut_limit, 1.0 - cut_ratio * cut_ratio, 0.0)
    return jnp.concatenate([damping, damping], axis=0)


def analyze(state_grid_field, fourier_basis_table):
    return jnp.einsum("hpu,pa->hau", state_grid_field, fourier_basis_table, precision=TOP_PRECISION)


def rebuild(fourier_spectra, fourier_basis_table):
    return jnp.einsum(
        "zum,gu->zgm", fourier_spectra, fourier_basis_table, precision=TOP_PRECISION
    ) * (2.0 / LONGITUDE_COUNT)


def diffuse(state_grid_field, diffusivity, zonal_row_weight):
    cycle_padded = padded(state_grid_field, (("lon", 1),), 1, True)
    band_padded = padded(state_grid_field, (("lat", 2),), 1, False)
    zonal_term = cycle_padded[:, 2:, :] + cycle_padded[:, :-2, :] - 2.0 * state_grid_field
    meridional = band_padded[:, :, 2:] + band_padded[:, :, :-2] - 2.0 * state_grid_field
    return diffusivity[:, None, None] * (zonal_row_weight[None, None, :] * zonal_term + meridional)


def summed_spectra(polar_slab, fourier_basis_table):
    local_spectra = analyze(polar_slab, fourier_basis_table)
    return lax.psum(local_spectra, "lon")


def cycle_filter(polar_slab, weight_set, fourier_basis_table):
    fourier_spectra = summed_spectra(polar_slab, fourier_basis_table)
    filtered = polar_slab - rebuild(fourier_spectra * weight_set[None], fourier_basis_table)
    return (filtered,)


def per_device(
    background_state,
    perturbation,
    surface_pattern_index,
    surface_amplitude_table,
    cutoff,
    zonal_row_weight,
    diffusivity,
    input_weight,
    bias,
    output_weight,
):
    lon_dev = background_state.shape[1]
    lat_dev = background_state.shape[2]
    pattern_values = jnp.arange(surface_amplitude_table.shape[0], dtype=jnp.int32)
    surface_field = jnp.sum(
        jnp.where(
            surface_pattern_index[None] == pattern_values[:, None, None],
            surface_amplitude_table[:, None, None],
            0.0,
        ),
        axis=0,
    )
    start_pert = perturbation.astype(jnp.float32)
    perturbation_field = jnp.concatenate(
        [start_pert[:1] + surface_field[None], start_pert[1:]], axis=0
    )
    before_activation = (
        jnp.einsum(
            "vb,bqf->vqf", input_weight, background_state, preferred_element_type=jnp.float32
        )
        + bias[:, None, None]
    )
    active = jnp.tanh(before_activation)
    activation_slope = 1.0 - active * active
    wide_weight = input_weight.astype(jnp.float32)
    hidden_forward = (
        jnp.einsum("vb,bqf->vqf", wide_weight, perturbation_field, precision=TOP_PRECISION)
        * activation_slope
    )
    tangent_image = (
        perturbation_field
        + diffuse(perturbation_field, diffusivity, zonal_row_weight)
        + 0.5 * jnp.einsum("sm,mxq->sxq", output_weight, hidden_forward, precision=TOP_PRECISION)
    )
    last_band = lax.axis_index("lat") == lax.axis_size("lat") - 1

    def orient(values_in):
        return jnp.where(last_band, jnp.flip(values_in, axis=-1), values_in)

    slab_start = jnp.where(last_band, lat_dev - POLAR, 0).astype(jnp.int32)
    polar_cut = orient(lax.dynamic_slice_in_dim(cutoff, slab_start, POLAR, 0))
    weight_set = removal_weights(polar_cut)
    longitudes = lax.axis_index("lon") * lon_dev + jnp.arange(lon_dev, dtype=jnp.int32)
    fourier_basis_table = spectral_table(longitudes)

    def spectral(polar_slab):
        return cycle_filter(polar_slab, weight_set, fourier_basis_table)

    polar_slab = orient(lax.dynamic_slice_in_dim(tangent_image, slab_start, POLAR, 2))
    filtered = spectral(polar_slab)[0]
    tangent_full = lax.dynamic_update_slice_in_dim(tangent_image, orient(filtered), slab_start, 2)
    twice = spectral(orient(lax.dynamic_slice_in_dim(tangent_full, slab_start, POLAR, 2)))[0]
    adjoint_input = lax.dynamic_update_slice_in_dim(tangent_full, orient(twice), slab_start, 2)
    hidden_backward = (
        jnp.einsum("xf,xbe->fbe", output_weight, adjoint_input, precision=TOP_PRECISION)
        * activation_slope
    )
    gradient = (
        adjoint_input
        + diffuse(adjoint_input, diffusivity, zonal_row_weight)
        + 0.5 * jnp.einsum("zo,zmf->omf", wide_weight, hidden_backward, precision=TOP_PRECISION)
    )
    return (tangent_full.astype(jnp.bfloat16), gradient.astype(jnp.bfloat16))


def solution(mesh):
    placed = (
        P(None, "lon", "lat"),
        P(None, "lon", "lat"),
        P("lon", "lat"),
        P(),
        P("lat"),
        P("lat"),
        P(),
        P(),
        P(),
        P(),
    )
    return jax.shard_map(
        per_device,
        mesh=mesh,
        in_specs=placed,
        out_specs=(P(None, "lon", "lat"), P(None, "lon", "lat")),
        check_vma=False,
    )
```

profile of v0, /device:TPU:1, one launch (start us, length us, event | category | flops | bytes accessed | tf_op | source)
XLA Modules:
  0.0 1695.8 jit_solution(2790603785789324412)
XLA Ops:
  11.9 1.5 fusion.2
  13.4 1.6 copy.59
  15.0 16.6 collective-permute-start
  31.9 1.9 collective-permute-start.1
  33.9 2.9 collective-permute-start.2
  36.8 3.0 collective-permute-start.3
  39.9 1.5 copy.63
  41.4 3.7 fusion.45
  45.1 1.9 fusion.27
  47.3 4.0 fusion.1
  51.4 1.5 copy.65
  55.8 3.2 fusion.19
  61.7 762.4 %all-reduce.3.cloned.1.call-done = f32[18,128,64]{1,2,0:T(8,128)} async-done(((f32[18,128,64]{1,2,0:T(8,128)}), f32[18,128,64]{1,2,0:T(8,128)}) %all-reduce.3.cloned.1.call-update) | async-done | bytes 589840 | tf_op jit(solution)/shard_map/psum | solution.py:61
  829.7 789.7 %all-reduce.5.cloned.1.call-done = f32[18,128,64]{1,2,0:T(8,128)} async-done(((f32[18,128,64]{1,2,0:T(8,128)}), f32[18,128,64]{1,2,0:T(8,128)}) %all-reduce.5.cloned.1.call-update) | async-done | bytes 589840 | tf_op jit(solution)/shard_map/psum | solution.py:61
  1621.7 1.5 copy.70
  1624.7 3.3 fusion.38
  1628.0 1.6 copy.66
  1629.6 9.5 collective-permute-start.4
  1639.5 1.9 collective-permute-start.5
  1641.4 32.0 %collective-permute-start.6 = (f32[18,90,1]{1,2,0:T(1,128)S(1)}, f32[18,90,1]{1,2,0:T(1,128)S(1)}, u32[]{:S(2)}, u32[]{:S(2)}) collective-permute-start(f32[18,90,1]{1,2,0:T(1,128)S(1)} %get-tuple-element.14), channel_id=1, source_target_pairs={{64,0},{128,64},{192,128},{256,192},{320,256},{384,320},{448,384},... | collective-permute-start | bytes 19448 | tf_op jit(solution)/shard_map/ppermute | solution.py:21
  1673.4 2.3 collective-permute-start.7
  1675.7 4.6 fusion
  1680.3 1.6 copy.71
  1684.8 3.0 fusion.10
  (79 shorter events, 24.6 us)
Async XLA Ops:
  7.2 37.9 %copy-start = (bf16[18,90,128]{2,1,0:T(8,128)(2,1)S(1)}, bf16[18,90,128]{2,1,0:T(8,128)(2,1)}, u32[]{:S(2)}) copy-start(bf16[18,90,128]{2,1,0:T(8,128)(2,1)} %param.10) | copy-start | bytes 1244164
  7.2 817.0 %all-reduce.3.cloned.1.call-start = ((), (), s32[]{:S(2)}) async-start(), calls=%async_computation | async-start | bytes 1179648 | tf_op jit(solution)/shard_map/psum | solution.py:61
  9.8 0.8 copy-start.4
  9.8 0.8 copy-start.8
  15.0 37.9 %collective-permute-start = (f32[18,1,128]{2,1,0:T(1,128)S(1)}, f32[18,1,128]{2,1,0:T(1,128)S(1)}, u32[]{:S(2)}, u32[]{:S(2)}) collective-permute-start(f32[18,1,128]{2,1,0:T(1,128)S(1)} %copy.59), channel_id=1, source_target_pairs={{1,0},{2,1},{3,2},{4,3},{5,4},{6,5},{7,6},{8,7},{9,8},{10,9},{11,1... | collective-permute-start | bytes 27656 | tf_op jit(solution)/shard_map/ppermute | solution.py:21
  31.9 22.4 %collective-permute-start.1 = (f32[18,1,128]{2,1,0:T(1,128)S(1)}, f32[18,1,128]{2,1,0:T(1,128)S(1)}, u32[]{:S(2)}, u32[]{:S(2)}) collective-permute-start(f32[18,1,128]{2,1,0:T(1,128)S(1)} %copy.61), channel_id=1, source_target_pairs={{0,1},{1,2},{2,3},{3,4},{4,5},{5,6},{6,7},{7,8},{8,9},{9,10},{10,1... | collective-permute-start | bytes 27656 | tf_op jit(solution)/shard_map/ppermute | solution.py:20
  33.9 21.9 %collective-permute-start.2 = (f32[18,90,1]{1,2,0:T(1,128)S(1)}, f32[18,90,1]{1,2,0:T(1,128)S(1)}, u32[]{:S(2)}, u32[]{:S(2)}) collective-permute-start(f32[18,90,1]{1,2,0:T(1,128)S(1)} %get-tuple-element.18), channel_id=1, source_target_pairs={{64,0},{128,64},{192,128},{256,192},{320,256},{384,320},{448,384},... | collective-permute-start | bytes 19448 | tf_op jit(solution)/shard_map/ppermute | solution.py:21
  36.8 19.0 %collective-permute-start.3 = (f32[18,90,1]{1,2,0:T(1,128)S(1)}, f32[18,90,1]{1,2,0:T(1,128)S(1)}, u32[]{:S(2)}, u32[]{:S(2)}) collective-permute-start(f32[18,90,1]{1,2,0:T(1,128)S(1)} %get-tuple-element.19), channel_id=1, source_target_pairs={{0,64},{64,128},{128,192},{192,256},{256,320},{320,384},{384,448},... | collective-permute-start | bytes 19448 | tf_op jit(solution)/shard_map/ppermute | solution.py:20
  39.9 1.5 copy-start.2
  45.1 2.2 copy-start.3
  45.1 2.2 copy-start.5
  52.9 2.9 copy-start.6
  52.9 2.9 copy-start.7
  59.6 1.7 copy-start.9
  61.1 1558.3 %all-reduce.5.cloned.1.call-start = ((), (), s32[]{:S(2)}) async-start(), calls=%async_computation.1 | async-start | bytes 1179648 | tf_op jit(solution)/shard_map/psum | solution.py:61
  1623.2 1.5 copy-start.1
  1629.6 52.4 %collective-permute-start.4 = (f32[18,1,128]{2,1,0:T(1,128)S(1)}, f32[18,1,128]{2,1,0:T(1,128)S(1)}, u32[]{:S(2)}, u32[]{:S(2)}) collective-permute-start(f32[18,1,128]{2,1,0:T(1,128)S(1)} %copy.66), channel_id=1, source_target_pairs={{1,0},{2,1},{3,2},{4,3},{5,4},{6,5},{7,6},{8,7},{9,8},{10,9},{11,1... | collective-permute-start | bytes 27656 | tf_op jit(solution)/shard_map/ppermute | solution.py:21
  1639.5 43.9 %collective-permute-start.5 = (f32[18,1,128]{2,1,0:T(1,128)S(1)}, f32[18,1,128]{2,1,0:T(1,128)S(1)}, u32[]{:S(2)}, u32[]{:S(2)}) collective-permute-start(f32[18,1,128]{2,1,0:T(1,128)S(1)} %copy.68), channel_id=1, source_target_pairs={{0,1},{1,2},{2,3},{3,4},{4,5},{5,6},{6,7},{7,8},{8,9},{9,10},{10,1... | collective-permute-start | bytes 27656 | tf_op jit(solution)/shard_map/ppermute | solution.py:20
  1641.4 43.4 %collective-permute-start.6 = (f32[18,90,1]{1,2,0:T(1,128)S(1)}, f32[18,90,1]{1,2,0:T(1,128)S(1)}, u32[]{:S(2)}, u32[]{:S(2)}) collective-permute-start(f32[18,90,1]{1,2,0:T(1,128)S(1)} %get-tuple-element.14), channel_id=1, source_target_pairs={{64,0},{128,64},{192,128},{256,192},{320,256},{384,320},{448,384},... | collective-permute-start | bytes 19448 | tf_op jit(solution)/shard_map/ppermute | solution.py:21
  1673.4 11.4 collective-permute-start.7
Sparse Core Ops, SparseCore 0:
  61.2 762.9 all-reduce.2
  828.6 790.6 all-reduce.4
where the time goes:
time: 1700 us
  waiting for transfers between devices  1550 us (91%)
  starting transfers between devices  70.3 us (4%)
  local copies, waits for them, and re-layouts  23.7 us (1%)
  matrix products  21.6 us (1%)
    psum x2, waiting for transfers between devices, summed_spectra(): return lax.psum(local_spectra, 'lon')  1550 us
    ppermute x4, starting transfers between devices, padded(): after = lax.ppermute(leading, axis, down)  61 us
  transfers between devices with their start and end apart: 10, of which 2 were waited for; matrix products, arithmetic and copies ran while one was open for 2% of the time, Pallas kernels for 0%

commit v1 on v0

--- a/solution.py
+++ b/solution.py
@@ -8,6 +8,11 @@
 KW = 64
 POLAR = 64
 TOP_PRECISION = lax.Precision.HIGHEST
+
+
+def gather_and_add(block, mesh_axis):
+    terms = lax.all_gather(block, mesh_axis)
+    return jnp.sum(terms, axis=0)
 
 
 def padded(x, sides, width, wrap):
@@ -58,7 +63,7 @@
 
 def summed_spectra(polar_slab, fourier_basis_table):
     local_spectra = analyze(polar_slab, fourier_basis_table)
-    return lax.psum(local_spectra, "lon")
+    return gather_and_add(local_spectra, "lon")
 
 
 def cycle_filter(polar_slab, weight_set, fourier_basis_table):

time: 1700 us -> 1250 us (0.74)
  waiting for transfers between devices: 1550 us -> 1110 us
  starting transfers between devices: 70.3 us -> 43.3 us
  other arithmetic: 13.6 us -> 37.9 us
    psum x2 -> x0, waiting for transfers between devices: 1550 us -> none  [summed_spectra(): return lax.psum(local_spectra, 'lon')]
    all_gather x0 -> x2, waiting for transfers between devices: none -> 1110 us  [gather_and_add(): terms = lax.all_gather(block, mesh_axis)]
    reduce_sum x0 -> x2, other arithmetic: none -> 26.4 us  [gather_and_add(): return jnp.sum(terms, axis=0)]
    ppermute x4, starting transfers between devices: 61 us -> 34.8 us  [padded(): after = lax.ppermute(leading, axis, down)]
where the time goes in v1:
time: 1250 us
  waiting for transfers between devices  1110 us (89%)
  starting transfers between devices  43.3 us (3%)
  other arithmetic  37.9 us (3%)
  local copies, waits for them, and re-layouts  23.1 us (2%)
  matrix products  16.5 us (1%)
  between operations  14.5 us (1%)
    all_gather x2, waiting for transfers between devices, gather_and_add(): terms = lax.all_gather(block, mesh_axis)  1110 us
    ppermute x4, starting transfers between devices, padded(): after = lax.ppermute(leading, axis, down)  34.8 us
    reduce_sum x2, other arithmetic, gather_and_add(): return jnp.sum(terms, axis=0)  26.4 us
  transfers between devices with their start and end apart: 10, of which 2 were waited for; matrix products, arithmetic and copies ran while one was open for 2% of the time, Pallas kernels for 0%

profile of v1, /device:TPU:1, one launch (start us, length us, event | category | flops | bytes accessed | tf_op | source)
XLA Modules:
  0.0 1246.5 jit_solution(17627779570735654853)
XLA Ops:
  11.3 8.8 collective-permute-start.2
  20.0 1.9 collective-permute-start.3
  23.4 1.6 copy.65
  25.1 1.9 collective-permute-start.1
  27.4 11.5 collective-permute-start
  39.0 1.5 copy.67
  40.5 2.3 fusion.45
  43.7 1.7 fusion.1
  45.5 1.5 copy.69
  49.9 3.2 fusion.19
  55.9 555.0 %all-gather.5.cloned.1.call-done = f32[1152,128,64]{1,2,0:T(8,128)} async-done(((f32[18,128,64]{1,2,0:T(8,128)}), f32[1152,128,64]{1,2,0:T(8,128)}) %all-gather.5.cloned.1.call-update) | async-done | bytes 37748752 | tf_op jit(solution)/shard_map/all_gather | solution.py:14
  610.9 13.2 %reduce_sum.28 = f32[18,128,64]{1,2,0:T(8,128)S(1)} reduce(f32[64,18,128,64]{2,3,1,0:T(8,128)} %bitcast.60, f32[]{:T(128)} %constant.15.clone.1), dimensions={0}, to_apply=%region_1.2 | reduce | flops 9289728 | bytes 38338564 | tf_op jit(solution)/shard_map/reduce_sum | solution.py:15
  628.6 556.0 %all-gather.7.cloned.1.call-done = f32[1152,128,64]{1,2,0:T(8,128)} async-done(((f32[18,128,64]{1,2,0:T(8,128)}), f32[1152,128,64]{1,2,0:T(8,128)}) %all-gather.7.cloned.1.call-update) | async-done | bytes 37748752 | tf_op jit(solution)/shard_map/all_gather | solution.py:14
  1184.6 13.2 %reduce_sum.29 = f32[18,128,64]{1,2,0:T(8,128)S(1)} reduce(f32[64,18,128,64]{2,3,1,0:T(8,128)} %bitcast.61, f32[]{:T(128)} %constant.15.clone.1), dimensions={0}, to_apply=%region_2.3 | reduce | flops 9289728 | bytes 38338564 | tf_op jit(solution)/shard_map/reduce_sum | solution.py:15
  1199.1 1.5 copy.74
  1202.1 3.0 collective-permute-start.6
  1205.1 2.6 collective-permute-start.7
  1207.7 3.3 fusion.38
  1211.0 1.6 copy.70
  1213.0 1.9 collective-permute-start.5
  1214.9 11.5 collective-permute-start.4
  1226.4 4.6 fusion
  1231.0 1.6 copy.75
  1235.6 3.1 fusion.10
  (85 shorter events, 23.8 us)
Async XLA Ops:
  7.2 35.7 %copy-start = (bf16[18,90,128]{2,1,0:T(8,128)(2,1)S(1)}, bf16[18,90,128]{2,1,0:T(8,128)(2,1)}, u32[]{:S(2)}) copy-start(bf16[18,90,128]{2,1,0:T(8,128)(2,1)} %param.10) | copy-start | bytes 1244164
  7.2 603.7 %all-gather.5.cloned.1.call-start = ((), (), s32[]{:S(2)}) async-start(), calls=%async_computation | async-start | bytes 38338560 | tf_op jit(solution)/shard_map/all_gather | solution.py:14
  8.7 1.2 copy-start.6
  8.7 1.2 copy-start.10
  11.3 38.7 %collective-permute-start.2 = (f32[18,90,1]{1,2,0:T(1,128)S(1)}, f32[18,90,1]{1,2,0:T(1,128)S(1)}, u32[]{:S(2)}, u32[]{:S(2)}) collective-permute-start(f32[18,90,1]{1,2,0:T(1,128)S(1)} %get-tuple-element.18), channel_id=1, source_target_pairs={{64,0},{128,64},{192,128},{256,192},{320,256},{384,320},{448,384},... | collective-permute-start | bytes 19448 | tf_op jit(solution)/shard_map/ppermute | solution.py:26
  20.0 29.9 %collective-permute-start.3 = (f32[18,90,1]{1,2,0:T(1,128)S(1)}, f32[18,90,1]{1,2,0:T(1,128)S(1)}, u32[]{:S(2)}, u32[]{:S(2)}) collective-permute-start(f32[18,90,1]{1,2,0:T(1,128)S(1)} %get-tuple-element.19), channel_id=1, source_target_pairs={{0,64},{64,128},{128,192},{192,256},{256,320},{320,384},{384,448},... | collective-permute-start | bytes 19448 | tf_op jit(solution)/shard_map/ppermute | solution.py:25
  25.1 23.4 %collective-permute-start.1 = (f32[18,1,128]{2,1,0:T(1,128)S(1)}, f32[18,1,128]{2,1,0:T(1,128)S(1)}, u32[]{:S(2)}, u32[]{:S(2)}) collective-permute-start(f32[18,1,128]{2,1,0:T(1,128)S(1)} %copy.65), channel_id=1, source_target_pairs={{0,1},{1,2},{2,3},{3,4},{4,5},{5,6},{6,7},{7,8},{8,9},{9,10},{10,1... | collective-permute-start | bytes 27656 | tf_op jit(solution)/shard_map/ppermute | solution.py:25
  27.4 19.7 %collective-permute-start = (f32[18,1,128]{2,1,0:T(1,128)S(1)}, f32[18,1,128]{2,1,0:T(1,128)S(1)}, u32[]{:S(2)}, u32[]{:S(2)}) collective-permute-start(f32[18,1,128]{2,1,0:T(1,128)S(1)} %copy.63), channel_id=1, source_target_pairs={{1,0},{2,1},{3,2},{4,3},{5,4},{6,5},{7,6},{8,7},{9,8},{10,9},{11,1... | collective-permute-start | bytes 27656 | tf_op jit(solution)/shard_map/ppermute | solution.py:26
  39.0 1.6 copy-start.4
  42.9 0.8 copy-start.5
  42.9 0.8 copy-start.7
  43.4 2.0 copy-start.2
  47.0 2.9 copy-start.8
  47.0 2.9 copy-start.9
  53.7 1.7 copy-start.11
  55.2 1129.4 %all-gather.7.cloned.1.call-start = ((), (), s32[]{:S(2)}) async-start(), calls=%async_computation.1 | async-start | bytes 38338560 | tf_op jit(solution)/shard_map/all_gather | solution.py:14
  1200.7 7.0 copy-start.3
  1202.1 33.4 %collective-permute-start.6 = (f32[18,90,1]{1,2,0:T(1,128)S(1)}, f32[18,90,1]{1,2,0:T(1,128)S(1)}, u32[]{:S(2)}, u32[]{:S(2)}) collective-permute-start(f32[18,90,1]{1,2,0:T(1,128)S(1)} %get-tuple-element.14), channel_id=1, source_target_pairs={{64,0},{128,64},{192,128},{256,192},{320,256},{384,320},{448,384},... | collective-permute-start | bytes 19448 | tf_op jit(solution)/shard_map/ppermute | solution.py:26
  1205.1 30.4 %collective-permute-start.7 = (f32[18,90,1]{1,2,0:T(1,128)S(1)}, f32[18,90,1]{1,2,0:T(1,128)S(1)}, u32[]{:S(2)}, u32[]{:S(2)}) collective-permute-start(f32[18,90,1]{1,2,0:T(1,128)S(1)} %get-tuple-element.15), channel_id=1, source_target_pairs={{0,64},{64,128},{128,192},{192,256},{256,320},{320,384},{384,448},... | collective-permute-start | bytes 19448 | tf_op jit(solution)/shard_map/ppermute | solution.py:25
  1213.0 21.1 %collective-permute-start.5 = (f32[18,1,128]{2,1,0:T(1,128)S(1)}, f32[18,1,128]{2,1,0:T(1,128)S(1)}, u32[]{:S(2)}, u32[]{:S(2)}) collective-permute-start(f32[18,1,128]{2,1,0:T(1,128)S(1)} %copy.72), channel_id=1, source_target_pairs={{0,1},{1,2},{2,3},{3,4},{4,5},{5,6},{6,7},{7,8},{8,9},{9,10},{10,1... | collective-permute-start | bytes 27656 | tf_op jit(solution)/shard_map/ppermute | solution.py:25
  1214.9 17.7 %collective-permute-start.4 = (f32[18,1,128]{2,1,0:T(1,128)S(1)}, f32[18,1,128]{2,1,0:T(1,128)S(1)}, u32[]{:S(2)}, u32[]{:S(2)}) collective-permute-start(f32[18,1,128]{2,1,0:T(1,128)S(1)} %copy.70), channel_id=1, source_target_pairs={{1,0},{2,1},{3,2},{4,3},{5,4},{6,5},{7,6},{8,7},{9,8},{10,9},{11,1... | collective-permute-start | bytes 27656 | tf_op jit(solution)/shard_map/ppermute | solution.py:26
  1235.6 4.1 copy-start.1
Sparse Core Ops, SparseCore 0:
  55.3 555.5 all-gather.4
  627.6 557.0 all-gather.6
